TPU v7x, 512 devices: a whole 4x8x8 slice. The times are simulated.
512 devices in a mesh: dp: 64 (over z, y), heads: 8 (over x, core).
Axes of the slice: x: 4, y: 8, z: 8, core: 2. Of those that a mesh axis runs over, the one named last changes fastest.
Arguments:
- queries: bfloat16 [64, 128, 8192], P('dp', 'heads'), may hold values from -6 to 6
- out_grad: bfloat16 [64, 128, 8192], P('dp', 'heads'), may hold values from -6 to 6
- q_gain: float32 [128], replicated, may hold values from 0.25 to 1.75
- k_gain: float32 [128], replicated, may hold values from 0.25 to 1.75
- image_keys: bfloat16 [64, 6464, 1024], P(None, 'dp', 'heads'), may hold values from -6 to 6
- image_values: bfloat16 [64, 6464, 1024], P(None, 'dp', 'heads'), may hold values from -48 to 48
- image_tiles: int32 [64], replicated, may hold values from 1 to 4, as said below
- text_len: int32 [64], replicated, may hold values from 1 to 128, as said below
Outputs:
- attention: bfloat16 [64, 128, 8192], P('dp', 'heads')
- query_grad: bfloat16 [64, 128, 8192], P('dp', 'heads')
Inputs may be any that keep to these rules, and one draw needn't show every extreme that they name: `image_tiles`: the tile counts of samples 4i to 4i+3 sum to 8, and some sample has 4 tiles. `text_len`: some sample has 128 live rows.
All inputs are finite; a program needn't handle non-finite values.
Results may differ from a plain program's by a relative error of at most 0.019.
Values may be sent and summed in bfloat16 or wider, within the bound.
A program may use at most 128 MiB of HBM per device.

v0:
```python
import jax
import jax.numpy as jnp
from jax import lax
from jax.sharding import PartitionSpec as P

TILE = 1601


EPSILON = 1e-05


def normalize(inputs, gain, factor):
    mean_sq = jnp.mean(inputs * inputs, axis=-1, keepdims=True)
    return inputs * lax.rsqrt(mean_sq + EPSILON) * gain * factor


def lookup(table, position):
    matched = jnp.arange(table.shape[0], dtype=jnp.int32) == position
    return jnp.sum(jnp.where(matched, table, 0))


def key_blocks(key_rows, value_rows, owners, live_limit, n_steps):
    n_owners = key_rows.shape[0]
    kcap_rows = key_rows.shape[1]
    block_len = n_owners // n_steps * kcap_rows
    key_block = key_rows.reshape((n_steps, block_len) + key_rows.shape[2:])
    value_block = value_rows.reshape((n_steps, block_len) + value_rows.shape[2:])
    token_ids = owners[:, None] * kcap_rows + jnp.arange(kcap_rows, dtype=jnp.int32)[None, :]
    live_mask = token_ids.reshape(n_steps, block_len) < live_limit
    live_count = jnp.sum(jnp.any(live_mask, axis=1).astype(jnp.int32))
    return (key_block, value_block, live_mask, live_count)


def block_weights(query_norm, key_now, live_now):
    scores = jnp.einsum("tkgd,jkd->tkgj", query_norm, key_now, preferred_element_type=jnp.float32)
    return jnp.where(live_now, jnp.exp(scores), 0.0).astype(jnp.bfloat16)


def forward_loop(query_norm, blocks):
    key_block, value_block, live_mask, live_count = blocks
    n_steps = key_block.shape[0]
    block_len = key_block.shape[1]

    def forward_advance(block_index, running):
        totals, summed, stored = running
        key_now = lax.dynamic_index_in_dim(key_block, block_index, 0, keepdims=False)
        value_now = lax.dynamic_index_in_dim(value_block, block_index, 0, keepdims=False)
        live_now = lax.dynamic_index_in_dim(live_mask, block_index, 0, keepdims=False)
        weights = block_weights(query_norm, key_now, live_now)
        totals = totals + jnp.sum(weights, axis=-1, dtype=jnp.float32)
        summed = summed + jnp.einsum(
            "tkgj,jkd->tkgd", weights, value_now, preferred_element_type=jnp.float32
        )
        stored = lax.dynamic_update_index_in_dim(stored, weights, block_index, 0)
        return (totals, summed, stored)

    initial = (
        jnp.zeros(query_norm.shape[:3], jnp.float32),
        jnp.zeros(query_norm.shape, jnp.float32),
        jnp.zeros((n_steps,) + query_norm.shape[:3] + (block_len,), jnp.bfloat16),
    )
    return lax.fori_loop(0, live_count, forward_advance, initial)


def backward_loop(grad_rows, blocks, stored, totals, deltas):
    key_block, value_block, live_mask, live_count = blocks

    def backward_advance(block_index, running):
        key_now = lax.dynamic_index_in_dim(key_block, block_index, 0, keepdims=False)
        value_now = lax.dynamic_index_in_dim(value_block, block_index, 0, keepdims=False)
        weights = lax.dynamic_index_in_dim(stored, block_index, 0, keepdims=False)
        prob_grad = jnp.einsum(
            "tkgd,jkd->tkgj", grad_rows, value_now, preferred_element_type=jnp.float32
        )
        score_grad = (
            weights.astype(jnp.float32) * (prob_grad - deltas[..., None]) / totals[..., None]
        ).astype(jnp.bfloat16)
        return running + jnp.einsum(
            "tkgj,jkd->tkgd", score_grad, key_now, preferred_element_type=jnp.float32
        )

    return lax.fori_loop(0, live_count, backward_advance, jnp.zeros(grad_rows.shape, jnp.float32))


def local(queries, out_grad, q_gain, k_gain, image_keys, image_values, image_tiles, text_len):
    n_devices = lax.axis_size("dp")
    my_index = lax.axis_index("dp")
    head_dim = q_gain.shape[0]
    q_scale = head_dim ** (-0.5)
    samples, kcap_rows, key_width = image_keys.shape
    key_heads = key_width // head_dim
    split_rows, split_grads = (
        lax.all_to_all(queries, "heads", split_axis=2, concat_axis=1, tiled=True),
        lax.all_to_all(out_grad, "heads", split_axis=2, concat_axis=1, tiled=True),
    )
    text_rows = split_rows.shape[1]
    features = split_rows.shape[2]
    q_group = features // key_width
    raw_rows = split_rows[0].astype(jnp.float32).reshape(text_rows, key_heads, q_group, head_dim)
    query_norm = normalize(raw_rows, q_gain, q_scale).astype(jnp.bfloat16)
    length = lookup(text_len, my_index)
    row_live = (jnp.arange(text_rows, dtype=jnp.int32) < length)[:, None, None, None]
    grad_rows = jnp.where(
        row_live,
        split_grads[0].reshape(text_rows, key_heads, q_group, head_dim),
        jnp.zeros((), jnp.bfloat16),
    )
    key_norm = normalize(
        image_keys.astype(jnp.float32).reshape(samples, kcap_rows, key_heads, head_dim), k_gain, 1.0
    ).astype(jnp.bfloat16)
    value_rows = image_values.reshape(samples, kcap_rows, key_heads, head_dim)
    fetched_keys, fetched_values = (
        lax.all_to_all(key_norm, "dp", split_axis=0, concat_axis=1, tiled=True),
        lax.all_to_all(value_rows, "dp", split_axis=0, concat_axis=1, tiled=True),
    )
    fetched_keys = fetched_keys[0].reshape(n_devices, kcap_rows, key_heads, head_dim)
    fetched_values = fetched_values[0].reshape(n_devices, kcap_rows, key_heads, head_dim)
    my_tiles = lookup(image_tiles, my_index)
    all_blocks = key_blocks(
        fetched_keys, fetched_values, jnp.arange(n_devices, dtype=jnp.int32), my_tiles * TILE, 8
    )
    totals, summed, stored = forward_loop(query_norm, all_blocks)
    attended = jnp.where(row_live, summed / totals[..., None], 0.0)
    deltas = jnp.sum(grad_rows.astype(jnp.float32) * attended, axis=-1)
    attention = attended.astype(jnp.bfloat16).reshape(1, text_rows, features)
    attention = lax.all_to_all(attention, "heads", split_axis=1, concat_axis=2, tiled=True)
    norm_grad = backward_loop(grad_rows, all_blocks, stored, totals, deltas)
    pullback = jax.vjp(lambda inputs: normalize(inputs, q_gain, q_scale), raw_rows)[1]
    query_grad = pullback(norm_grad)[0].astype(jnp.bfloat16).reshape(1, text_rows, features)
    query_grad = lax.all_to_all(query_grad, "heads", split_axis=1, concat_axis=2, tiled=True)
    return (attention, query_grad)


def solution(mesh):
    return jax.shard_map(
        local,
        mesh=mesh,
        in_specs=(
            P("dp", "heads", None),
            P("dp", "heads", None),
            P(),
            P(),
            P(None, "dp", "heads"),
            P(None, "dp", "heads"),
            P(),
            P(),
        ),
        out_specs=(P("dp", "heads", None), P("dp", "heads", None)),
        check_vma=False,
    )
```

profile of v0, /device:TPU:24, one launch (start us, length us, event | category | flops | bytes accessed | tf_op | source)
XLA Modules:
  0.0 339.0 jit_solution(6407234425520808682)
XLA Ops:
  0.6 8.3 %copy.103 = bf16[1,16,8192]{1,0,2:T(2,128)(2,1)} copy(bf16[1,16,8192]{2,1,0:T(8,128)(2,1)} %param.12) | data formatting | bytes 524288 | tf_op args[0]
  9.5 45.3 %reduce.9 = bf16[8192,16]{1,0:T(8,128)(2,1)S(1)} reduce(bf16[8192,1,16]{2,1,0:T(2,128)(2,1)} %bitcast.196, bf16[]{:T(256)} %broadcast.160), dimensions={1}, to_apply=%bitcast.145.reduce_sub_computation | reduce | bytes 524290
  54.8 2.8 reshape.244
  57.7 4.3 %all-to-all-start.1 = ((bf16[8,2,8192]{2,1,0:T(2,128)(2,1)}), bf16[8,2,8192]{2,1,0:T(2,128)(2,1)S(1)}, u32[]{:S(2)}, u32[]{:S(2)}) async-start(bf16[8,2,8192]{2,1,0:T(2,128)(2,1)} %reshape.244), calls=%async_computation.1 | async-start | bytes 524288 | tf_op jit(solution)/shard_map/all_to_all | solution.py:93
  62.0 3.0 fusion.36
  64.9 6.7 %copy.113 = bf16[1,16,8192]{1,0,2:T(2,128)(2,1)} copy(bf16[1,16,8192]{2,1,0:T(8,128)(2,1)S(1)} %copy-done) | data formatting | bytes 524288 | tf_op args[1]
  71.6 45.3 %reduce.10 = bf16[8192,16]{1,0:T(8,128)(2,1)S(1)} reduce(bf16[8192,1,16]{2,1,0:T(2,128)(2,1)} %bitcast.199, bf16[]{:T(256)} %broadcast.160), dimensions={1}, to_apply=%bitcast.149.reduce_sub_computation | reduce | bytes 524290
  116.9 2.8 reshape.248
  119.8 4.8 %all-to-all-start.4 = ((bf16[8,2,8192]{2,1,0:T(2,128)(2,1)}), bf16[8,2,8192]{2,1,0:T(2,128)(2,1)S(1)}, u32[]{:S(2)}, u32[]{:S(2)}) async-start(bf16[8,2,8192]{2,1,0:T(2,128)(2,1)} %reshape.248), calls=%async_computation.4 | async-start | bytes 524288 | tf_op jit(solution)/shard_map/all_to_all | solution.py:94
  124.6 3.2 fusion.39
  127.8 4.3 %all-to-all-done.4 = bf16[8,2,8192]{2,1,0:T(2,128)(2,1)S(1)} async-done(((bf16[8,2,8192]{2,1,0:T(2,128)(2,1)}), bf16[8,2,8192]{2,1,0:T(2,128)(2,1)S(1)}, u32[]{:S(2)}, u32[]{:S(2)}) %all-to-all-start.4) | async-done | bytes 262176 | tf_op jit(solution)/shard_map/all_to_all | solution.py:94
  132.1 16.4 %all-to-all-start = ((bf16[64,101,1,128]{3,1,2,0:T(8,128)(2,1)}), bf16[64,101,1,128]{3,1,2,0:T(8,128)(2,1)S(1)}, u32[]{:S(2)}, u32[]{:S(2)}) async-start(bf16[64,101,1,128]{3,1,2,0:T(8,128)(2,1)} %fusion.39), calls=%async_computation | async-start | bytes 3407872 | tf_op jit(solution)/shard_map/all_to_all | solution.py:113
  148.5 3.8 %copy.134 = bf16[64,101,128]{2,1,0:T(8,128)(2,1)} copy(bf16[64,101,128]{2,0,1:T(8,128)(2,1)} %param.17) | data formatting | bytes 3309568 | tf_op args[5]
  152.3 38.8 %all-to-all-done = bf16[64,101,1,128]{3,1,2,0:T(8,128)(2,1)S(1)} async-done(((bf16[64,101,1,128]{3,1,2,0:T(8,128)(2,1)}), bf16[64,101,1,128]{3,1,2,0:T(8,128)(2,1)S(1)}, u32[]{:S(2)}, u32[]{:S(2)}) %all-to-all-start) | async-done | bytes 1654816 | tf_op jit(solution)/shard_map/all_to_all | solution.py:113
  191.1 8.3 %all-to-all-start.2 = ((bf16[64,101,1,128]{3,1,2,0:T(8,128)(2,1)}), bf16[64,101,1,128]{3,1,2,0:T(8,128)(2,1)}, u32[]{:S(2)}, u32[]{:S(2)}) async-start(bf16[64,101,1,128]{3,1,2,0:T(8,128)(2,1)} %bitcast.204), calls=%async_computation.2 | async-start | bytes 3407872 | tf_op jit(solution)/shard_map/all_to_all | solution.py:114
  203.1 5.1 %reshape.245 = bf16[8192,1,16]{2,1,0:T(2,128)(2,1)} reshape(bf16[8,2,8192]{2,1,0:T(2,128)(2,1)S(1)} %all-to-all-done.1) | data formatting | bytes 524288
  208.2 8.4 %bitcast_convert_fusion = f32[1,16,8192]{1,0,2:T(1,128)} fusion(bf16[8192,1,16]{2,1,0:T(2,128)(2,1)} %reshape.245), kind=kLoop, calls=%fused_computation.63 | loop fusion | flops 131072 | bytes 786432 | tf_op jit(solution)/shard_map/convert_element_type | solution.py:99
  216.6 3.7 %copy.104 = f32[1,16,8,1024]{3,0,1,2:T(1,128)S(1)} copy(f32[1,16,8,1024]{1,3,2,0:T(8,128)} %bitcast.197) | data formatting | bytes 1048576 | tf_op jit(solution)/shard_map/convert_element_type | solution.py:99
  221.6 5.1 %reshape.249 = bf16[8192,1,16]{2,1,0:T(2,128)(2,1)} reshape(bf16[8,2,8192]{2,1,0:T(2,128)(2,1)S(1)} %all-to-all-done.4) | data formatting | bytes 524288
  226.7 7.9 %copy.114 = bf16[1,16,8192]{2,1,0:T(8,128)(2,1)S(1)} copy(bf16[1,16,8192]{1,0,2:T(2,128)(2,1)} %bitcast.198) | data formatting | bytes 524288 | tf_op jit(solution)/shard_map/all_to_all | solution.py:94
  237.5 3.1 all-to-all-done.2
  243.1 6.4 %broadcast_in_dim.62 = bf16[8,128,1,8,808]{1,4,3,2,0:T(8,128)(2,1)} broadcast(bf16[]{:T(256)} %constant.59.clone.1), dimensions={} | broadcast | bytes 13238274 | tf_op jit(solution)/shard_map/broadcast_in_dim | solution.py:60
  249.6 35.1 %while.24 = (s32[]{:T(128)}, f32[128,1,8]{0,2,1:T(8,128)S(1)}, f32[128,1,8,128]{0,3,2,1:T(8,128)S(1)}, bf16[8,128,1,8,808]{1,4,3,2,0:T(8,128)(2,1)}, s32[]{:T(12...) while((s32[]{:T(128)}, f32[128,1,8]{0,2,1:T(8,128)S(1)}, ...), condition=%wide.region_8.9_spmd, body=%wide.region_6.8_spmd.sunk | while | flops 427065344 | bytes 8362535 | solution.py:62
  289.0 3.4 %all-to-all-start.3 = ((bf16[8,2,8192]{2,1,0:T(2,128)(2,1)}), bf16[8,2,8192]{2,1,0:T(2,128)(2,1)S(1)}, u32[]{:S(2)}, u32[]{:S(2)}) async-start(bf16[8,2,8192]{2,1,0:T(2,128)(2,1)} %reshape.246), calls=%async_computation.3 | async-start | bytes 524288 | tf_op jit(solution)/shard_map/all_to_all | solution.py:126
  292.4 27.1 %while.25 = (s32[]{:T(128)}, f32[128,1,8,128]{0,3,2,1:T(8,128)S(1)}, s32[]{:T(128)}, bf16[8,808,1,128]{3,1,2,0:T(8,128)(2,1)}, bf16[8,128,1,8,808]{1,4,3,2,0:T(8...) while((s32[]{:T(128)}, ...), condition=%wide.region_11.12_spmd, body=%wide.region_10.11_spmd.sunk | while | flops 427892736 | bytes 3389087 | solution.py:82
  293.1 2.6 fusion.61
  296.4 2.6 fusion.61
  299.6 2.6 fusion.61
  306.2 2.6 fusion.61
  312.7 2.6 fusion.61
  325.6 4.7 %all-to-all-start.5 = ((bf16[8,2,8192]{2,1,0:T(2,128)(2,1)}), bf16[8,2,8192]{2,1,0:T(2,128)(2,1)S(1)}, u32[]{:S(2)}, u32[]{:S(2)}) async-start(bf16[8,2,8192]{2,1,0:T(2,128)(2,1)} %reshape.250), calls=%async_computation.5 | async-start | bytes 524288 | tf_op jit(solution)/shard_map/all_to_all | solution.py:130
  331.4 6.5 %all-to-all-done.5 = bf16[8,2,8192]{2,1,0:T(2,128)(2,1)S(1)} async-done(((bf16[8,2,8192]{2,1,0:T(2,128)(2,1)}), bf16[8,2,8192]{2,1,0:T(2,128)(2,1)S(1)}, u32[]{:S(2)}, u32[]{:S(2)}) %all-to-all-start.5) | async-done | bytes 262176 | tf_op jit(solution)/shard_map/all_to_all | solution.py:130
  (109 shorter events, 59.7 us)
Async XLA Ops:
  54.8 10.1 %copy-start = (bf16[1,16,8192]{2,1,0:T(8,128)(2,1)S(1)}, bf16[1,16,8192]{2,1,0:T(8,128)(2,1)}, u32[]{:S(2)}) copy-start(bf16[1,16,8192]{2,1,0:T(8,128)(2,1)} %param.13) | copy-start | bytes 786436
  57.7 62.1 %all-to-all-start.1 = ((bf16[8,2,8192]{2,1,0:T(2,128)(2,1)}), bf16[8,2,8192]{2,1,0:T(2,128)(2,1)S(1)}, u32[]{:S(2)}, u32[]{:S(2)}) async-start(bf16[8,2,8192]{2,1,0:T(2,128)(2,1)} %reshape.244), calls=%async_computation.1 | async-start | bytes 524288 | tf_op jit(solution)/shard_map/all_to_all | solution.py:93
  71.6 53.0 %copy-start.6 = (f32[128]{0:T(128)S(1)}, f32[128]{0:T(128)}, u32[]{:S(2)}) copy-start(f32[128]{0:T(128)} %param.15) | copy-start | bytes 1540
  119.8 12.4 %all-to-all-start.4 = ((bf16[8,2,8192]{2,1,0:T(2,128)(2,1)}), bf16[8,2,8192]{2,1,0:T(2,128)(2,1)S(1)}, u32[]{:S(2)}, u32[]{:S(2)}) async-start(bf16[8,2,8192]{2,1,0:T(2,128)(2,1)} %reshape.248), calls=%async_computation.4 | async-start | bytes 524288 | tf_op jit(solution)/shard_map/all_to_all | solution.py:94
  132.1 59.0 %all-to-all-start = ((bf16[64,101,1,128]{3,1,2,0:T(8,128)(2,1)}), bf16[64,101,1,128]{3,1,2,0:T(8,128)(2,1)S(1)}, u32[]{:S(2)}, u32[]{:S(2)}) async-start(bf16[64,101,1,128]{3,1,2,0:T(8,128)(2,1)} %fusion.39), calls=%async_computation | async-start | bytes 3407872 | tf_op jit(solution)/shard_map/all_to_all | solution.py:113
  148.5 51.2 %copy-start.4 = (s32[64]{0:T(128)S(1)}, s32[64]{0:T(128)}, u32[]{:S(2)}) copy-start(s32[64]{0:T(128)} %param.19) | copy-start | bytes 772
  148.5 51.2 %copy-start.5 = (s32[64]{0:T(128)S(1)}, s32[64]{0:T(128)}, u32[]{:S(2)}) copy-start(s32[64]{0:T(128)} %param.18) | copy-start | bytes 772
  148.5 54.1 %copy-start.3 = (f32[128]{0:T(128)S(1)}, f32[128]{0:T(128)}, u32[]{:S(2)}) copy-start(f32[128]{0:T(128)} %param.14) | copy-start | bytes 1540
  191.1 49.5 %all-to-all-start.2 = ((bf16[64,101,1,128]{3,1,2,0:T(8,128)(2,1)}), bf16[64,101,1,128]{3,1,2,0:T(8,128)(2,1)}, u32[]{:S(2)}, u32[]{:S(2)}) async-start(bf16[64,101,1,128]{3,1,2,0:T(8,128)(2,1)} %bitcast.204), calls=%async_computation.2 | async-start | bytes 3407872 | tf_op jit(solution)/shard_map/all_to_all | solution.py:114
  220.6 0.6 copy-start.2
  284.7 1.2 copy-start.1
  289.0 36.6 %all-to-all-start.3 = ((bf16[8,2,8192]{2,1,0:T(2,128)(2,1)}), bf16[8,2,8192]{2,1,0:T(2,128)(2,1)S(1)}, u32[]{:S(2)}, u32[]{:S(2)}) async-start(bf16[8,2,8192]{2,1,0:T(2,128)(2,1)} %reshape.246), calls=%async_computation.3 | async-start | bytes 524288 | tf_op jit(solution)/shard_map/all_to_all | solution.py:126
  325.6 12.2 %all-to-all-start.5 = ((bf16[8,2,8192]{2,1,0:T(2,128)(2,1)}), bf16[8,2,8192]{2,1,0:T(2,128)(2,1)S(1)}, u32[]{:S(2)}, u32[]{:S(2)}) async-start(bf16[8,2,8192]{2,1,0:T(2,128)(2,1)} %reshape.250), calls=%async_computation.5 | async-start | bytes 524288 | tf_op jit(solution)/shard_map/all_to_all | solution.py:130
where the time goes:
time: 342 us; the launch traced here: 339 us
  other arithmetic  116 us (34%)
  local copies, waits for them, and re-layouts  75.4 us (22%)
  waiting for transfers between devices  52.7 us (15%)
  starting transfers between devices  41.9 us (12%)
  matrix products  39.3 us (11%)
  loops' own time  12.1 us (4%)
    unnamed x4, other arithmetic  94.9 us
    all_to_all x1, waiting for transfers between devices, local(): lax.all_to_all(key_norm, 'dp', split_axis=0, concat_axis=1, tiled=True)  38.8 us
    unnamed x30, local copies, waits for them, and re-layouts  38.6 us
    dot_general x8, matrix products, backward_advance(): jnp.einsum('tkgj,jkd->tkgd', score_grad, key_now, preferred_element_type=...  21 us
    all_to_all x1, starting transfers between devices, local(): lax.all_to_all(key_norm, 'dp', split_axis=0, concat_axis=1, tiled=True)  16.4 us
    dot_general x8, matrix products, block_weights(): jnp.einsum('tkgd,jkd->tkgj', query_norm, key_now, preferred_element_type=...  14.3 us
    dynamic_update_slice x8, local copies, waits for them, and re-layouts, forward_advance(): stored = lax.dynamic_update_index_in_dim(stored, weights, block_index, 0)  10.5 us
    convert_element_type x1, other arithmetic, local(): split_rows[0].astype(jnp.float32)  8.43 us
  transfers between devices with their start and end apart: 6, of which 4 were waited for; matrix products, arithmetic and copies ran while one was open for 38% of the time, Pallas kernels for 0%

commit v1 on v0

v1 whole, which is shorter than its diff:
```python
import functools

import jax
import jax.numpy as jnp
from jax import lax
from jax.experimental import pallas as pl
from jax.experimental.pallas import tpu as pltpu
from jax.sharding import PartitionSpec as P

MESH = pl.DeviceIdType.MESH
EPSILON = 1e-05
TILE = 1601
HD = 128
GQ = 8
ROWS = 104
N = 8
Z_ORDER = (1, 7, 2, 6, 3, 5, 4)
Y_ORDER = (1, 7, 3, 5)
E_ORDER = (2, 6, 4)
BLOCK_ORDER = (0, 1, 7, 2, 6, 4, 3, 5)
NT = (((1,), (1,)), ((), ()))
GROUP = 256


def kernel(slots, tiles_ref, len_ref, q_ref, g_ref, qg_ref, kg_ref, p_ref, att_ref, grad_ref,
           qb, gb, i1, i2, fin, own, vk, qn, gm, acc_a, acc_b, acc_c, acc_t, ao, go,
           qs, qr, gs, gr, s1zs, s1zr, s1ys, s1yr, s2ys, s2yr, s2zs, s2zr, oas, oar, ogs, ogr, loc):
    dp = lax.axis_index("dp")
    h = lax.axis_index("heads")
    z, y = dp // N, dp % N
    par, half = y % 2, y // 2

    def zz(d):
        return (z + d) % N

    def yy(d):
        return (y + d) % N

    def at(dz, dy):
        return (zz(dz) * N + yy(dy), h)

    def hh(d):
        return (h + d) % N

    def remote(src, dst, ssem, rsem, dev):
        copy = pltpu.make_async_remote_copy(
            src_ref=src, dst_ref=dst, send_sem=ssem, recv_sem=rsem, device_id=dev, device_id_type=MESH)
        copy.start()
        return copy

    barrier = pltpu.get_barrier_semaphore()
    for d in range(1, N):
        for dev in (at(d, 0), at(0, d), (dp, hh(d))):
            pl.semaphore_signal(barrier, inc=1, device_id=dev, device_id_type=MESH)
    pl.semaphore_wait(barrier, 3 * (N - 1))

    width = GQ * HD

    def cols(i):
        return pl.ds(pl.multiple_of(i * width, width), width)

    c1 = {}
    order = (("z", 1), ("y", 1), ("z", 7), ("z", 2), ("y", 7), ("z", 6), ("z", 3), ("y", 3), ("z", 5), ("z", 4), ("y", 5))
    sent = []
    for kind, d in order:
        if kind == "z":
            c1[kind, d] = remote(p_ref.at[zz(d), par], i1.at[d - 1], s1zs.at[d - 1], s1zr.at[d - 1], at(d, 0))
        else:
            c1[kind, d] = remote(p_ref.at[:, yy(d) % 2, yy(d) // 2], i2.at[d // 2], s1ys.at[d // 2], s1yr.at[d // 2], at(0, d))
        sent.append(c1[kind, d])
    cq = []
    for d in range(1, N):
        cq.append(remote(q_ref.at[0, :, cols(hh(d))], qb.at[h], qs.at[d - 1], qr.at[d - 1], (dp, hh(d))))
        cq.append(remote(g_ref.at[0, :, cols(hh(d))], gb.at[h], gs.at[d - 1], gr.at[d - 1], (dp, hh(d))))
    sent += cq
    locals_ = [
        pltpu.make_async_copy(q_ref.at[0, :, cols(h)], qb.at[h], loc.at[0]),
        pltpu.make_async_copy(g_ref.at[0, :, cols(h)], gb.at[h], loc.at[1]),
        pltpu.make_async_copy(p_ref.at[z, par, half], own, loc.at[2]),
    ]
    for copy in locals_:
        copy.start()

    c2 = {}

    def forward_y(dz):
        for dy in E_ORDER:
            src = p_ref.at[z, par, yy(dy) // 2] if dz == 0 else i1.at[dz - 1, yy(dy) // 2]
            i = dy // 2 - 1
            c2[dy, dz] = remote(src, fin.at[i, dz], s2ys.at[i, dz], s2yr.at[i, dz], at(0, dy))
            sent.append(c2[dy, dz])

    def forward_z(dy):
        i = dy // 2
        for dz in Z_ORDER:
            c2[dy, dz] = remote(i2.at[i, zz(dz)], fin.at[3 + i, dz], s2zs.at[i, dz - 1], s2zr.at[i, dz - 1], at(dz, 0))
            sent.append(c2[dy, dz])

    forward_y(0)

    for copy in locals_:
        copy.wait()
    for copy in cq:
        copy.wait_recv()
    length = len_ref[dp]
    limit = tiles_ref[dp] * TILE
    row_live = lax.broadcasted_iota(jnp.int32, (N * 16, HD), 0) < length
    q_gain = qg_ref[...] * (HD ** -0.5)

    def raw(ref, g):
        return ref[:, :, g * HD:(g + 1) * HD].reshape(N * 16, HD).astype(jnp.float32)

    for g in range(GQ):
        here = slice(g * N * 16, (g + 1) * N * 16)
        q = raw(qb, g)
        mean_sq = jnp.mean(q * q, axis=-1, keepdims=True)
        qn[here, :] = (q * lax.rsqrt(mean_sq + EPSILON) * q_gain).astype(jnp.bfloat16)
        gm[here, :] = jnp.where(row_live, raw(gb, g), 0.0).astype(jnp.bfloat16)
    for ref in (acc_a, acc_b, acc_c, acc_t):
        ref[...] = jnp.zeros_like(ref)

    for kind, d in order:
        c1[kind, d].wait_recv()
        if kind == "z":
            forward_y(d)
        else:
            forward_z(d)

    k_gain = kg_ref[...]
    width_b = N * ROWS
    lane = lax.broadcasted_iota(jnp.int32, (1, width_b), 1)
    lane_dz = lane // ROWS
    lane_j = lane % ROWS

    def block(dy):
        chunks = []
        for dz in range(N):
            if dy == 0:
                chunks.append(own[...] if dz == 0 else i1[dz - 1, half])
            elif dy % 2 == 0:
                c2[dy, dz].wait_recv()
                chunks.append(fin[dy // 2 - 1, dz])
            elif dz == 0:
                chunks.append(i2[dy // 2, z])
            else:
                c2[dy, dz].wait_recv()
                chunks.append(fin[3 + dy // 2, dz])
        for i in range(0, N, 2):
            both = jnp.concatenate([chunks[i].astype(jnp.float32), chunks[i + 1].astype(jnp.float32)], axis=0)
            k = both[:, :HD]
            mean_sq = jnp.mean(k * k, axis=-1, keepdims=True)
            k = k * lax.rsqrt(mean_sq + EPSILON) * k_gain
            vk[i * ROWS:(i + 2) * ROWS, :HD] = both[:, HD:].astype(jnp.bfloat16)
            vk[i * ROWS:(i + 2) * ROWS, HD:] = k.astype(jnp.bfloat16)
        source = ((z - lane_dz + N) % N) * N + (y - dy + N) % N
        live = ((lane_j < slots) & (source * slots + lane_j < limit)).astype(jnp.float32)

        def rows(r, carry):
            here = pl.ds(pl.multiple_of(r * GROUP, GROUP), GROUP)
            q, g = qn[here, :], gm[here, :]
            s = lax.dot_general(q, vk[:, HD:], NT, preferred_element_type=jnp.float32)
            w = (jnp.exp(s) * live).astype(jnp.bfloat16)
            ac = jnp.dot(w, vk[...], preferred_element_type=jnp.float32)
            wf = w.astype(jnp.float32)
            a = acc_a[here, :] + ac[:, :HD]
            t = acc_t[here, :] + jnp.sum(wf, axis=-1, keepdims=True)
            d0 = jnp.sum(g.astype(jnp.float32) * a, axis=-1, keepdims=True) / jnp.maximum(t[:, :1], 1e-30)
            pg = lax.dot_general(g, vk[:, :HD], NT, preferred_element_type=jnp.float32)
            p = (wf * (pg - d0)).astype(jnp.bfloat16)
            b = jnp.dot(p, vk[:, HD:], preferred_element_type=jnp.float32)
            acc_a[here, :] = a
            acc_t[here, :] = t
            acc_b[here, :] = acc_b[here, :] + b + d0 * ac[:, HD:]
            acc_c[here, :] = acc_c[here, :] + ac[:, HD:]
            return carry

        lax.fori_loop(0, N * 16 * GQ // GROUP, rows, 0)

    for dy in BLOCK_ORDER:
        block(dy)

    for g in range(GQ):
        here = slice(g * N * 16, (g + 1) * N * 16)
        there = slice(g * HD, (g + 1) * HD)
        t = acc_t[here, :]
        att = jnp.where(row_live, acc_a[here, :] / t, 0.0)
        ao[:, :, there] = att.astype(jnp.bfloat16).reshape(N, 16, HD)
        delta = jnp.sum(gm[here, :].astype(jnp.float32) * att, axis=-1, keepdims=True)
        norm_grad = (acc_b[here, :] - delta * acc_c[here, :]) / t
        q = raw(qb, g)
        r = lax.rsqrt(jnp.mean(q * q, axis=-1, keepdims=True) + EPSILON)
        u = norm_grad * q_gain
        dq = r * u - q * (r * r * r * jnp.mean(q * u, axis=-1, keepdims=True))
        go[:, :, there] = dq.astype(jnp.bfloat16).reshape(N, 16, HD)
    outs = []
    for d in range(1, N):
        outs.append(remote(ao.at[hh(d)], att_ref.at[0, :, cols(h)], oas.at[d - 1], oar.at[d - 1], (dp, hh(d))))
        outs.append(remote(go.at[hh(d)], grad_ref.at[0, :, cols(h)], ogs.at[d - 1], ogr.at[d - 1], (dp, hh(d))))
    mine = [
        pltpu.make_async_copy(ao.at[h], att_ref.at[0, :, cols(h)], loc.at[0]),
        pltpu.make_async_copy(go.at[h], grad_ref.at[0, :, cols(h)], loc.at[1]),
    ]
    for copy in mine:
        copy.start()
    for copy in sent:
        copy.wait_send()
    for copy in mine:
        copy.wait()
    for copy in outs:
        copy.wait()


def local(queries, out_grad, q_gain, k_gain, image_keys, image_values, image_tiles, text_len):
    samples, slots, _ = image_keys.shape
    both = jnp.concatenate([image_keys, image_values], axis=-1)
    both = jnp.pad(both, ((0, 0), (0, ROWS - slots), (0, 0)))
    packed = both.reshape(N, N // 2, 2, ROWS, 2 * HD).transpose(0, 2, 1, 3, 4)
    rows = queries.shape[1] * N
    q_rows = rows * GQ
    bf, f32 = jnp.bfloat16, jnp.float32
    dma = pltpu.SemaphoreType.DMA
    vmem = pl.BlockSpec(memory_space=pltpu.VMEM)
    smem = pl.BlockSpec(memory_space=pltpu.SMEM)
    hbm = pl.BlockSpec(memory_space=pl.ANY)
    out = jax.ShapeDtypeStruct(queries.shape, bf)

    return tuple(pl.pallas_call(
        functools.partial(kernel, slots),
        name="exchange_attention",
        out_shape=(out, out),
        in_specs=[smem, smem, hbm, hbm, vmem, vmem, hbm],
        out_specs=(hbm, hbm),
        scratch_shapes=[
            pltpu.VMEM((N, 16, GQ * HD), bf),
            pltpu.VMEM((N, 16, GQ * HD), bf),
            pltpu.VMEM((7, 4, ROWS, 2 * HD), bf),
            pltpu.VMEM((4, N, ROWS, 2 * HD), bf),
            pltpu.VMEM((7, N, ROWS, 2 * HD), bf),
            pltpu.VMEM((ROWS, 2 * HD), bf),
            pltpu.VMEM((N * ROWS, 2 * HD), bf),
            pltpu.VMEM((q_rows, HD), bf),
            pltpu.VMEM((q_rows, HD), bf),
            pltpu.VMEM((q_rows, HD), f32),
            pltpu.VMEM((q_rows, HD), f32),
            pltpu.VMEM((q_rows, HD), f32),
            pltpu.VMEM((q_rows, HD), f32),
            pltpu.VMEM((N, 16, GQ * HD), bf),
            pltpu.VMEM((N, 16, GQ * HD), bf),
            dma((7,)), dma((7,)), dma((7,)), dma((7,)),
            dma((7,)), dma((7,)), dma((4,)), dma((4,)),
            dma((3, N)), dma((3, N)), dma((4, 7)), dma((4, 7)),
            dma((7,)), dma((7,)), dma((7,)), dma((7,)),
            dma((3,)),
        ],
        compiler_params=pltpu.CompilerParams(
            collective_id=0, has_side_effects=True, vmem_limit_bytes=48 * 2 ** 20),
        cost_estimate=pl.CostEstimate(flops=8_000_000_000, bytes_accessed=8_000_000, transcendentals=7_000_000),
    )(image_tiles, text_len, queries, out_grad, q_gain.reshape(1, HD), k_gain.reshape(1, HD), packed))


def solution(mesh):
    return jax.shard_map(
        local,
        mesh=mesh,
        in_specs=(
            P("dp", "heads", None),
            P("dp", "heads", None),
            P(),
            P(),
            P(None, "dp", "heads"),
            P(None, "dp", "heads"),
            P(),
            P(),
        ),
        out_specs=(P("dp", "heads", None), P("dp", "heads", None)),
        check_vma=False,
    )
```

time: 342 us -> 127 us (0.37)
  the two profiles are of different devices: /device:TPU:24 before, /device:TPU:1 now
where the time goes in v1:
time: 127 us; the launch traced here: 126 us
  Pallas kernels  119 us (94%)
  local copies, waits for them, and re-layouts  6.11 us (5%)
    pallas_call x1, Pallas kernels, local(): pl.pallas_call(functools.partial(kernel, slots), name='exchange_attention...  119 us
    unnamed x18, local copies, waits for them, and re-layouts  5.76 us

profile of v1, /device:TPU:1, one launch (start us, length us, event | category | flops | bytes accessed | tf_op | source)
XLA Modules:
  0.0 126.4 jit_solution(729401719065010847)
XLA Ops:
  0.6 0.0 copy-start.6
  0.6 2.6 %copy.10 = bf16[64,101,128]{2,1,0:T(8,128)(2,1)S(1)} copy(bf16[64,101,128]{2,0,1:T(8,128)(2,1)} %param.12) | data formatting | bytes 3309568 | tf_op args[4]
  3.3 0.0 copy-done.6
  3.3 1.1 copy.11
  4.4 0.4 fusion.2
  4.8 0.0 copy-start
  4.8 0.0 copy-start.1
  4.8 0.0 copy-start.2
  4.8 0.0 copy-start.3
  4.8 0.0 copy-start.4
  4.8 0.0 copy-start.5
  4.9 0.3 copy.14
  5.2 0.5 copy-done
  5.7 0.1 copy-done.1
  5.8 0.0 copy-done.2
  5.8 0.0 copy-done.3
  5.8 0.0 copy-done.4
  5.8 0.0 copy-done.5
  5.8 119.2 %exchange_attention.1 = (bf16[1,16,8192]{2,1,0:T(8,128)(2,1)S(1)}, bf16[1,16,8192]{2,1,0:T(8,128)(2,1)S(1)}) custom-call(s32[64]{0:T(128)S(1)} %copy-done.2, s32[64]{0:T(128)S(1)} %copy-done.3, bf16[1,16,8192]{2,1,0:T(8,128)(2,1)S(1)} %copy-done, bf16[1,16,8192]{2,1,0:T(8,128)(2,1)S(1)} %copy-done.1, f32[1,128]{1,0:T(1,128)S(1)} %bitcast.7, ...), custom_call_target="tpu_custom_call" | custom-call | flops 8000000000 | bytes 8000000 | tf_op jit(solution)/shard_map/exchange_attention/pallas_call | solution.py:227
  125.0 0.7 copy.17
  125.7 0.7 copy.18
Async XLA Ops:
  0.6 2.6 %copy-start.6 = (bf16[64,101,128]{2,0,1:T(8,128)(2,1)S(1)}, bf16[64,101,128]{2,0,1:T(8,128)(2,1)}, u32[]{:S(2)}) copy-start(bf16[64,101,128]{2,0,1:T(8,128)(2,1)} %param.13) | copy-start | bytes 4964356
  4.8 1.0 copy-start
  4.8 1.0 copy-start.1
  4.8 1.0 copy-start.2
  4.8 1.0 copy-start.3
  4.8 1.0 copy-start.4
  4.8 1.0 copy-start.5

commit v2 on v1

--- a/solution.py
+++ b/solution.py
@@ -158,23 +158,26 @@
         def rows(r, carry):
             here = pl.ds(pl.multiple_of(r * GROUP, GROUP), GROUP)
             q, g = qn[here, :], gm[here, :]
+            a, t = acc_a[here, :], acc_t[here, :]
             s = lax.dot_general(q, vk[:, HD:], NT, preferred_element_type=jnp.float32)
             w = (jnp.exp(s) * live).astype(jnp.bfloat16)
+            pg = lax.dot_general(g, vk[:, :HD], NT, preferred_element_type=jnp.float32)
+            wf = w.astype(jnp.float32)
             ac = jnp.dot(w, vk[...], preferred_element_type=jnp.float32)
-            wf = w.astype(jnp.float32)
-            a = acc_a[here, :] + ac[:, :HD]
-            t = acc_t[here, :] + jnp.sum(wf, axis=-1, keepdims=True)
+            a_now = a + ac[:, :HD]
+            t_now = t + jnp.sum(wf, axis=-1, keepdims=True)
+            if dy == 0:
+                a, t = a_now, t_now
             d0 = jnp.sum(g.astype(jnp.float32) * a, axis=-1, keepdims=True) / jnp.maximum(t[:, :1], 1e-30)
-            pg = lax.dot_general(g, vk[:, :HD], NT, preferred_element_type=jnp.float32)
             p = (wf * (pg - d0)).astype(jnp.bfloat16)
             b = jnp.dot(p, vk[:, HD:], preferred_element_type=jnp.float32)
-            acc_a[here, :] = a
-            acc_t[here, :] = t
+            acc_a[here, :] = a_now
+            acc_t[here, :] = t_now
             acc_b[here, :] = acc_b[here, :] + b + d0 * ac[:, HD:]
             acc_c[here, :] = acc_c[here, :] + ac[:, HD:]
             return carry
 
-        lax.fori_loop(0, N * 16 * GQ // GROUP, rows, 0)
+        lax.fori_loop(0, N * 16 * GQ // GROUP, rows, 0, unroll=True)
 
     for dy in BLOCK_ORDER:
         block(dy)

time: 127 us -> 118 us (0.929)
  Pallas kernels: 119 us -> 110 us
    pallas_call x1, Pallas kernels: 119 us -> 110 us  [local(): pl.pallas_call(functools.partial(kernel, slots), name='exchange_attention...]
where the time goes in v2:
time: 118 us
  Pallas kernels  110 us (93%)
  local copies, waits for them, and re-layouts  6.11 us (5%)
    pallas_call x1, Pallas kernels, local(): pl.pallas_call(functools.partial(kernel, slots), name='exchange_attention...  110 us
    unnamed x18, local copies, waits for them, and re-layouts  5.76 us

profile of v2, /device:TPU:1, one launch (start us, length us, event | category | flops | bytes accessed | tf_op | source)
XLA Modules:
  0.0 117.7 jit_solution(232810695190951740)
XLA Ops:
  0.6 0.0 copy-start.6
  0.6 2.6 %copy.10 = bf16[64,101,128]{2,1,0:T(8,128)(2,1)S(1)} copy(bf16[64,101,128]{2,0,1:T(8,128)(2,1)} %param.12) | data formatting | bytes 3309568 | tf_op args[4]
  3.3 0.0 copy-done.6
  3.3 1.1 copy.11
  4.4 0.4 fusion.2
  4.8 0.0 copy-start
  4.8 0.0 copy-start.1
  4.8 0.0 copy-start.2
  4.8 0.0 copy-start.3
  4.8 0.0 copy-start.4
  4.8 0.0 copy-start.5
  4.9 0.3 copy.14
  5.2 0.5 copy-done
  5.7 0.1 copy-done.1
  5.8 0.0 copy-done.2
  5.8 0.0 copy-done.3
  5.8 0.0 copy-done.4
  5.8 0.0 copy-done.5
  5.8 110.4 %exchange_attention.1 = (bf16[1,16,8192]{2,1,0:T(8,128)(2,1)S(1)}, bf16[1,16,8192]{2,1,0:T(8,128)(2,1)S(1)}) custom-call(s32[64]{0:T(128)S(1)} %copy-done.2, s32[64]{0:T(128)S(1)} %copy-done.3, bf16[1,16,8192]{2,1,0:T(8,128)(2,1)S(1)} %copy-done, bf16[1,16,8192]{2,1,0:T(8,128)(2,1)S(1)} %copy-done.1, f32[1,128]{1,0:T(1,128)S(1)} %bitcast.7, ...), custom_call_target="tpu_custom_call" | custom-call | flops 8000000000 | bytes 8000000 | tf_op jit(solution)/shard_map/exchange_attention/pallas_call | solution.py:230
  116.3 0.7 copy.17
  117.0 0.7 copy.18
Async XLA Ops:
  0.6 2.6 %copy-start.6 = (bf16[64,101,128]{2,0,1:T(8,128)(2,1)S(1)}, bf16[64,101,128]{2,0,1:T(8,128)(2,1)}, u32[]{:S(2)}) copy-start(bf16[64,101,128]{2,0,1:T(8,128)(2,1)} %param.13) | copy-start | bytes 4964356
  4.8 1.0 copy-start
  4.8 1.0 copy-start.1
  4.8 1.0 copy-start.2
  4.8 1.0 copy-start.3
  4.8 1.0 copy-start.4
  4.8 1.0 copy-start.5

commit v3 on v2

v3 whole, which is shorter than its diff:
```python
import functools

import jax
import jax.numpy as jnp
from jax import lax
from jax.experimental import pallas as pl
from jax.experimental.pallas import tpu as pltpu
from jax.sharding import PartitionSpec as P

MESH = pl.DeviceIdType.MESH
EPSILON = 1e-05
TILE = 1601
HD = 128
GQ = 8
ROWS = 104
N = 8
SLABS = (1, 7, 2, 6, 3, 5, 4, 0)
READY = 2
FINAL = 2
PLAN = (
    ("send", 1), ("send", 7), ("send", 2), ("send", 6), ("rows", 0),
    ("forward", 1), ("forward", 7), ("send", 3), ("send", 5), ("send", 4),
    ("forward", 2), ("forward", 6), ("send", 0), ("attend", 1), ("attend", 7),
    ("forward", 3), ("forward", 5), ("attend", 2), ("attend", 6), ("forward", 4),
    ("attend", 3), ("attend", 5), ("attend", 0), ("attend", 4),
)
ODD = (1, 7, 3, 5)
EVEN = (2, 6, 4)
PARTS = 2
NT = (((1,), (1,)), ((), ()))
GROUP = 256


def kernel(slots, tiles_ref, len_ref, q_ref, g_ref, qg_ref, kg_ref, k_ref, v_ref, att_ref, grad_ref,
           kin, vin, pk, qb, gb, i1, i2, fin, vk, qn, gm, acc_a, acc_b, acc_c, acc_t, ao, go,
           qs, qr, gs, gr, s1zs, s1zr, s1ys, s1yr, s2ys, s2yr, s2zs, s2zr, oas, oar, ogs, ogr, kin_sem, vin_sem, loc):
    dp = lax.axis_index("dp")
    h = lax.axis_index("heads")
    z, y = dp // N, dp % N
    par, half = y % 2, y // 2

    def zz(d):
        return (z + d) % N

    def yy(d):
        return (y + d) % N

    def at(dz, dy):
        return (zz(dz) * N + yy(dy), h)

    def hh(d):
        return (h + d) % N

    def remote(src, dst, ssem, rsem, dev):
        copy = pltpu.make_async_remote_copy(
            src_ref=src, dst_ref=dst, send_sem=ssem, recv_sem=rsem, device_id=dev, device_id_type=MESH)
        copy.start()
        return copy

    width = GQ * HD

    def cols(i, part=0, parts=1):
        return pl.ds(pl.multiple_of(i * width + part * (width // parts), width // parts), width // parts)

    loads = {}
    for d in SLABS:
        loads[d] = (pltpu.make_async_copy(k_ref.at[:, zz(d)], kin.at[d], kin_sem.at[d]),
                    pltpu.make_async_copy(v_ref.at[:, zz(d)], vin.at[d], vin_sem.at[d]))
        for copy in loads[d]:
            copy.start()
    own = [
        pltpu.make_async_copy(q_ref.at[0, :, cols(h)], qb.at[h], loc.at[0]),
        pltpu.make_async_copy(g_ref.at[0, :, cols(h)], gb.at[h], loc.at[1]),
    ]
    for copy in own:
        copy.start()

    barrier = pltpu.get_barrier_semaphore()
    for d in range(1, N):
        for dev in (at(d, 0), at(0, d), (dp, hh(d))):
            pl.semaphore_signal(barrier, inc=1, device_id=dev, device_id_type=MESH)

    def pack(d):
        for copy in loads[d]:
            copy.wait()
        for ref, lanes in ((kin, slice(0, HD)), (vin, slice(HD, 2 * HD))):
            x = ref[d].astype(jnp.float32)
            x = jnp.concatenate([x, jnp.zeros((ROWS - slots,) + x.shape[1:], jnp.float32)], axis=0)
            x = jnp.swapaxes(x, 0, 1).astype(jnp.bfloat16)
            for i in range(N):
                pk[zz(d), i % 2, i // 2, :, lanes] = x[i]

    for d in SLABS[:READY]:
        pack(d)
    pl.semaphore_wait(barrier, 3 * (N - 1))

    sent = []
    cq = []
    for d in range(1, N):
        cq.append(remote(q_ref.at[0, :, cols(hh(d))], qb.at[h], qs.at[d - 1], qr.at[d - 1], (dp, hh(d))))
        cq.append(remote(g_ref.at[0, :, cols(hh(d))], gb.at[h], gs.at[d - 1], gr.at[d - 1], (dp, hh(d))))
    sent += cq

    c1z, c1y, c2 = {}, {}, {}

    def forward_y(dz):
        for dy in EVEN:
            src = pk.at[z, par, yy(dy) // 2] if dz == 0 else i1.at[dz - 1, yy(dy) // 2]
            i = dy // 2 - 1
            c2[dy, dz] = remote(src, fin.at[i, dz], s2ys.at[i, dz], s2yr.at[i, dz], at(0, dy))
            sent.append(c2[dy, dz])

    def forward_z(dy, dz):
        i = dy // 2
        c2[dy, dz] = remote(i2.at[i, zz(dz)], fin.at[3 + i, dz], s2zs.at[i, dz - 1], s2zr.at[i, dz - 1], at(dz, 0))
        sent.append(c2[dy, dz])

    def send(d):
        if d not in SLABS[:READY]:
            pack(d)
        if d:
            c1z[d] = remote(pk.at[zz(d), par], i1.at[d - 1], s1zs.at[d - 1], s1zr.at[d - 1], at(d, 0))
            sent.append(c1z[d])
        for dy in ODD:
            i = dy // 2
            c1y[dy, d] = remote(pk.at[zz(d), yy(dy) % 2, yy(dy) // 2], i2.at[i, zz(d)], s1ys.at[i, d], s1yr.at[i, d], at(0, dy))
            sent.append(c1y[dy, d])
        if d == 0:
            forward_y(0)

    def forward(d):
        c1z[d].wait_recv()
        forward_y(d)
        for dy in ODD:
            c1y[dy, d].wait_recv()
            forward_z(dy, d)

    length = len_ref[dp]
    limit = tiles_ref[dp] * TILE
    row_live = lax.broadcasted_iota(jnp.int32, (N * 16, HD), 0) < length
    q_gain = qg_ref[...] * (HD ** -0.5)

    def raw(ref, g):
        return ref[:, :, g * HD:(g + 1) * HD].reshape(N * 16, HD).astype(jnp.float32)

    def stage_rows():
        for copy in own:
            copy.wait()
        for copy in cq:
            copy.wait_recv()
        for g in range(GQ):
            here = slice(g * N * 16, (g + 1) * N * 16)
            q = raw(qb, g)
            mean_sq = jnp.mean(q * q, axis=-1, keepdims=True)
            qn[here, :] = (q * lax.rsqrt(mean_sq + EPSILON) * q_gain).astype(jnp.bfloat16)
            gm[here, :] = jnp.where(row_live, raw(gb, g), 0.0).astype(jnp.bfloat16)
        for ref in (acc_a, acc_b, acc_c, acc_t):
            ref[...] = jnp.zeros_like(ref)

    k_gain = kg_ref[...]
    width_b = N * ROWS
    lane = lax.broadcasted_iota(jnp.int32, (1, width_b), 1)
    lane_dy = lane // ROWS
    lane_j = lane % ROWS

    def stage(dz, slot=0):
        chunks = []
        for dy in range(N):
            if dz == 0 and dy % 2:
                c1y[dy, 0].wait_recv()
                chunks.append(i2[dy // 2, z])
            elif dy == 0:
                chunks.append(i1[dz - 1, half] if dz else pk[z, par, half])
            else:
                c2[dy, dz].wait_recv()
                chunks.append(fin[3 + dy // 2 if dy % 2 else dy // 2 - 1, dz])
        for i in range(0, N, 2):
            both = jnp.concatenate([chunks[i].astype(jnp.float32), chunks[i + 1].astype(jnp.float32)], axis=0)
            k = both[:, :HD]
            mean_sq = jnp.mean(k * k, axis=-1, keepdims=True)
            k = k * lax.rsqrt(mean_sq + EPSILON) * k_gain
            vk[slot, i * ROWS:(i + 2) * ROWS, :HD] = both[:, HD:].astype(jnp.bfloat16)
            vk[slot, i * ROWS:(i + 2) * ROWS, HD:] = k.astype(jnp.bfloat16)
        source = (z - dz + N) % N * N + (y - lane_dy + N) % N
        return ((lane_j < slots) & (source * slots + lane_j < limit)).astype(jnp.float32)

    def attend(live, first, last, shift_now, slot=0):
        def rows(r, carry):
            here = pl.ds(pl.multiple_of(r * GROUP, GROUP), GROUP)
            q, g = qn[here, :], gm[here, :]
            a, t = acc_a[here, :], acc_t[here, :]
            s = lax.dot_general(q, vk[slot, :, HD:], NT, preferred_element_type=jnp.float32)
            w = (jnp.exp(s) * live).astype(jnp.bfloat16)
            pg = lax.dot_general(g, vk[slot, :, :HD], NT, preferred_element_type=jnp.float32)
            wf = w.astype(jnp.float32)
            ac = jnp.dot(w, vk[slot], preferred_element_type=jnp.float32)
            a_now = a + ac[:, :HD]
            t_now = t + jnp.sum(wf, axis=-1, keepdims=True)
            if shift_now:
                a, t = a_now, t_now
            d0 = jnp.sum(g.astype(jnp.float32) * a, axis=-1, keepdims=True) / jnp.maximum(t[:, :1], 1e-30)
            p = (wf * (pg - d0)).astype(jnp.bfloat16)
            b = jnp.dot(p, vk[slot, :, HD:], preferred_element_type=jnp.float32)
            acc_a[here, :] = a_now
            acc_t[here, :] = t_now
            acc_b[here, :] = acc_b[here, :] + b + d0 * ac[:, HD:]
            acc_c[here, :] = acc_c[here, :] + ac[:, HD:]
            return carry

        lax.fori_loop(first, last, rows, 0, unroll=True)

    outs = []

    def finish(part):
        heads = GQ // PARTS
        for g in range(part * heads, (part + 1) * heads):
            here = slice(g * N * 16, (g + 1) * N * 16)
            there = slice(g * HD, (g + 1) * HD)
            t = acc_t[here, :]
            att = jnp.where(row_live, acc_a[here, :] / t, 0.0)
            ao[:, :, there] = att.astype(jnp.bfloat16).reshape(N, 16, HD)
            delta = jnp.sum(gm[here, :].astype(jnp.float32) * att, axis=-1, keepdims=True)
            norm_grad = (acc_b[here, :] - delta * acc_c[here, :]) / t
            q = raw(qb, g)
            r = lax.rsqrt(jnp.mean(q * q, axis=-1, keepdims=True) + EPSILON)
            u = norm_grad * q_gain
            dq = r * u - q * (r * r * r * jnp.mean(q * u, axis=-1, keepdims=True))
            go[:, :, there] = dq.astype(jnp.bfloat16).reshape(N, 16, HD)
        mine = pl.ds(part * heads * HD, heads * HD)
        for i, (buf, ref, ssem, rsem) in enumerate(((ao, att_ref, oas, oar), (go, grad_ref, ogs, ogr))):
            target = ref.at[0, :, cols(h, part, PARTS)]
            for d in range(1, N):
                outs.append(remote(buf.at[hh(d), :, mine], target, ssem.at[part, d - 1], rsem.at[part, d - 1], (dp, hh(d))))
            copy = pltpu.make_async_copy(buf.at[h, :, mine], target, loc.at[2 + 2 * part + i])
            copy.start()
            outs.append(copy)

    groups = N * 16 * GQ // GROUP
    attended = []
    for what, d in PLAN:
        if what == "send":
            send(d)
        elif what == "rows":
            stage_rows()
        elif what == "forward":
            forward(d)
        else:
            attended.append(d)
            if len(attended) + FINAL <= N:
                attend(stage(d), 0, groups, len(attended) <= 6)
    lives = {}
    for part in range(PARTS):
        for slot, d in enumerate(attended[N - FINAL:]):
            if part == 0:
                lives[d] = stage(d, slot)
            attend(lives[d], part * groups // PARTS, (part + 1) * groups // PARTS, False, slot)
        finish(part)
    for copy in sent:
        copy.wait_send()
    for copy in outs:
        copy.wait()


def place(a_ref, b_ref, x_ref, y_ref):
    x_ref[...] = a_ref[...]
    y_ref[...] = b_ref[...]


def local(queries, out_grad, q_gain, k_gain, image_keys, image_values, image_tiles, text_len):
    samples, slots, _ = image_keys.shape
    keys = image_keys.transpose(1, 0, 2).reshape(slots, N, N, HD)
    values = image_values.transpose(1, 0, 2).reshape(slots, N, N, HD)
    rows = queries.shape[1] * N
    q_rows = rows * GQ
    bf, f32 = jnp.bfloat16, jnp.float32
    dma = pltpu.SemaphoreType.DMA
    vmem = pl.BlockSpec(memory_space=pltpu.VMEM)
    smem = pl.BlockSpec(memory_space=pltpu.SMEM)
    hbm = pl.BlockSpec(memory_space=pl.ANY)
    out = jax.ShapeDtypeStruct(queries.shape, bf)

    attention, query_grad = pl.pallas_call(
        functools.partial(kernel, slots),
        name="exchange_attention",
        out_shape=(out, out),
        in_specs=[smem, smem, hbm, hbm, vmem, vmem, hbm, hbm],
        out_specs=(hbm, hbm),
        scratch_shapes=[
            pltpu.VMEM((N, slots, N, HD), bf),
            pltpu.VMEM((N, slots, N, HD), bf),
            pltpu.VMEM((N, 2, N // 2, ROWS, 2 * HD), bf),
            pltpu.VMEM((N, 16, GQ * HD), bf),
            pltpu.VMEM((N, 16, GQ * HD), bf),
            pltpu.VMEM((7, 4, ROWS, 2 * HD), bf),
            pltpu.VMEM((4, N, ROWS, 2 * HD), bf),
            pltpu.VMEM((7, N, ROWS, 2 * HD), bf),
            pltpu.VMEM((FINAL, N * ROWS, 2 * HD), bf),
            pltpu.VMEM((q_rows, HD), bf),
            pltpu.VMEM((q_rows, HD), bf),
            pltpu.VMEM((q_rows, HD), f32),
            pltpu.VMEM((q_rows, HD), f32),
            pltpu.VMEM((q_rows, HD), f32),
            pltpu.VMEM((q_rows, HD), f32),
            pltpu.VMEM((N, 16, GQ * HD), bf),
            pltpu.VMEM((N, 16, GQ * HD), bf),
            dma((7,)), dma((7,)), dma((7,)), dma((7,)),
            dma((7,)), dma((7,)), dma((4, N)), dma((4, N)),
            dma((3, N)), dma((3, N)), dma((4, 7)), dma((4, 7)),
            dma((PARTS, 7)), dma((PARTS, 7)), dma((PARTS, 7)), dma((PARTS, 7)),
            dma((N,)), dma((N,)), dma((2 + 2 * PARTS,)),
        ],
        compiler_params=pltpu.CompilerParams(
            collective_id=0, has_side_effects=True, vmem_limit_bytes=60 * 2 ** 20),
        cost_estimate=pl.CostEstimate(flops=8_000_000_000, bytes_accessed=8_000_000, transcendentals=7_000_000),
    )(image_tiles, text_len, queries, out_grad, q_gain.reshape(1, HD), k_gain.reshape(1, HD), keys, values)

    return tuple(pl.pallas_call(
        place,
        name="place_results",
        out_shape=(out, out),
        in_specs=[vmem, vmem],
        out_specs=(vmem, vmem),
        compiler_params=pltpu.CompilerParams(vmem_limit_bytes=60 * 2 ** 20),
    )(attention, query_grad))


def solution(mesh):
    return jax.shard_map(
        local,
        mesh=mesh,
        in_specs=(
            P("dp", "heads", None),
            P("dp", "heads", None),
            P(),
            P(),
            P(None, "dp", "heads"),
            P(None, "dp", "heads"),
            P(),
            P(),
        ),
        out_specs=(P("dp", "heads", None), P("dp", "heads", None)),
        check_vma=False,
    )
```

time: 118 us -> 111 us (0.941); the launches traced: 118 us -> 109 us
  local copies, waits for them, and re-layouts: 6.11 us -> 0 us
    unnamed x18 -> x0, local copies, waits for them, and re-layouts: 5.76 us -> none
    pallas_call x1, Pallas kernels: 110 us -> 107 us  [local(): pl.pallas_call(functools.partial(kernel, slots), name='exchange_attention...]
    pallas_call x0 -> x1, Pallas kernels: none -> 1.84 us  [local(): pl.pallas_call(place, name='place_results', out_shape=(out, out), in_spec...]
where the time goes in v3:
time: 111 us; the launch traced here: 109 us
  Pallas kernels  109 us (98%)
    pallas_call x1, Pallas kernels, local(): pl.pallas_call(functools.partial(kernel, slots), name='exchange_attention...  107 us

profile of v3, /device:TPU:1, one launch (start us, length us, event | category | flops | bytes accessed | tf_op | source)
XLA Modules:
  0.0 109.3 jit_solution(13365763165870267837)
XLA Ops:
  0.6 106.8 %exchange_attention.1 = (bf16[1,16,8192]{2,1,0:T(8,128)(2,1)}, bf16[1,16,8192]{2,1,0:T(8,128)(2,1)}) custom-call(s32[64]{0:T(128)} %tiles_ref.1, s32[64]{0:T(128)} %len_ref.1, bf16[1,16,8192]{2,1,0:T(8,128)(2,1)} %q_ref.1, bf16[1,16,8192]{2,1,0:T(8,128)(2,1)} %g_ref.1, f32[1,128]{1,0:T(1,128)} %bitcast.10, f32[1,128]{1,0:T(1,128)} %bitcast.11, ...), custom_call_target="tpu_custom_call" | custom-call | flops 8000000000 | bytes 8000000 | tf_op jit(solution)/shard_map/exchange_attention/pallas_call | solution.py:282
  107.4 1.8 %place_results.1 = (bf16[1,16,8192]{2,1,0:T(8,128)(2,1)}, bf16[1,16,8192]{2,1,0:T(8,128)(2,1)}) custom-call(bf16[1,16,8192]{2,1,0:T(8,128)(2,1)} %get-tuple-element.4.a_ref, bf16[1,16,8192]{2,1,0:T(8,128)(2,1)} %get-tuple-element.5.b_ref), custom_call_target="tpu_custom_call" | custom-call | tf_op jit(solution)/shard_map/place_results/pallas_call | solution.py:317

commit v4 on v3

--- a/solution.py
+++ b/solution.py
@@ -14,15 +14,15 @@
 GQ = 8
 ROWS = 104
 N = 8
-SLABS = (1, 7, 2, 6, 3, 5, 4, 0)
+SLABS = (1, 7, 2, 6, 0, 3, 5, 4)
 READY = 2
 FINAL = 2
 PLAN = (
-    ("send", 1), ("send", 7), ("send", 2), ("send", 6), ("rows", 0),
-    ("forward", 1), ("forward", 7), ("send", 3), ("send", 5), ("send", 4),
-    ("forward", 2), ("forward", 6), ("send", 0), ("attend", 1), ("attend", 7),
-    ("forward", 3), ("forward", 5), ("attend", 2), ("attend", 6), ("forward", 4),
-    ("attend", 3), ("attend", 5), ("attend", 0), ("attend", 4),
+    ("send", 1), ("send", 7), ("rows", 0), ("send", 2), ("send", 6), ("send", 0),
+    ("forward", 1), ("forward", 7), ("send", 3), ("send", 5), ("send", 4), ("norm", 0),
+    ("forward", 2), ("forward", 6), ("attend", 0), ("attend", 1), ("forward", 3), ("attend", 7),
+    ("forward", 5), ("attend", 2), ("forward", 4), ("attend", 6), ("attend", 3), ("attend", 5),
+    ("attend", 4),
 )
 ODD = (1, 7, 3, 5)
 EVEN = (2, 6, 4)
@@ -96,10 +96,13 @@
 
     sent = []
     cq = []
-    for d in range(1, N):
-        cq.append(remote(q_ref.at[0, :, cols(hh(d))], qb.at[h], qs.at[d - 1], qr.at[d - 1], (dp, hh(d))))
-        cq.append(remote(g_ref.at[0, :, cols(hh(d))], gb.at[h], gs.at[d - 1], gr.at[d - 1], (dp, hh(d))))
-    sent += cq
+
+    def send_rows():
+        for d in range(1, N):
+            cq.append(remote(q_ref.at[0, :, cols(hh(d))], qb.at[h], qs.at[d - 1], qr.at[d - 1], (dp, hh(d))))
+            cq.append(remote(g_ref.at[0, :, cols(hh(d))], gb.at[h], gs.at[d - 1], gr.at[d - 1], (dp, hh(d))))
+        sent.extend(cq)
+
 
     c1z, c1y, c2 = {}, {}, {}
 
@@ -241,6 +244,8 @@
         if what == "send":
             send(d)
         elif what == "rows":
+            send_rows()
+        elif what == "norm":
             stage_rows()
         elif what == "forward":
             forward(d)
@@ -253,7 +258,7 @@
         for slot, d in enumerate(attended[N - FINAL:]):
             if part == 0:
                 lives[d] = stage(d, slot)
-            attend(lives[d], part * groups // PARTS, (part + 1) * groups // PARTS, False, slot)
+            attend(lives[d], part * groups // PARTS, (part + 1) * groups // PARTS, slot + 1 < FINAL, slot)
         finish(part)
     for copy in sent:
         copy.wait_send()

time: 111 us -> 109 us (0.982)
  no operation moved by 1% of the time
where the time goes in v4:
time: 109 us; the launch traced here: 108 us
  Pallas kernels  108 us (99%)
    pallas_call x1, Pallas kernels, local(): pl.pallas_call(functools.partial(kernel, slots), name='exchange_attention...  106 us

profile of v4, /device:TPU:1, one launch (start us, length us, event | category | flops | bytes accessed | tf_op | source)
XLA Modules:
  0.0 108.2 jit_solution(350690462562083029)
XLA Ops:
  0.6 105.7 %exchange_attention.1 = (bf16[1,16,8192]{2,1,0:T(8,128)(2,1)}, bf16[1,16,8192]{2,1,0:T(8,128)(2,1)}) custom-call(s32[64]{0:T(128)} %tiles_ref.1, s32[64]{0:T(128)} %len_ref.1, bf16[1,16,8192]{2,1,0:T(8,128)(2,1)} %q_ref.1, bf16[1,16,8192]{2,1,0:T(8,128)(2,1)} %g_ref.1, f32[1,128]{1,0:T(1,128)} %bitcast.10, f32[1,128]{1,0:T(1,128)} %bitcast.11, ...), custom_call_target="tpu_custom_call" | custom-call | flops 8000000000 | bytes 8000000 | tf_op jit(solution)/shard_map/exchange_attention/pallas_call | solution.py:287
  106.4 1.8 %place_results.1 = (bf16[1,16,8192]{2,1,0:T(8,128)(2,1)}, bf16[1,16,8192]{2,1,0:T(8,128)(2,1)}) custom-call(bf16[1,16,8192]{2,1,0:T(8,128)(2,1)} %get-tuple-element.4.a_ref, bf16[1,16,8192]{2,1,0:T(8,128)(2,1)} %get-tuple-element.5.b_ref), custom_call_target="tpu_custom_call" | custom-call | tf_op jit(solution)/shard_map/place_results/pallas_call | solution.py:322
